TPU v7x, 32 devices: a whole 2x2x4 slice. The times are simulated.
32 devices in a mesh: layer: 2 (over y), dp: 16 (over z, x, core).
Axes of the slice: x: 2, y: 2, z: 4, core: 2. Of those that a mesh axis runs over, the one named last changes fastest.
Arguments:
- states: bfloat16 [6, 32, 32, 32, 128], P('layer', 'dp'), may hold values from -6 to 6
- weights: bfloat16 [6, 1152, 128], P('layer'), may hold values from -0.1875 to 0.1875
- bias: float32 [6, 128], P('layer'), may hold values from -3 to 3
- guesses: float32 [2, 32, 32, 32, 128], P('layer', 'dp'), may hold values from -6 to 6
- coarse_gain: float32 [2, 128], replicated, may hold values from 0.5 to 1
Outputs:
- section_starts: float32 [2, 32, 32, 32, 128], P('layer', 'dp')
- weight_grad: float32 [6, 1152, 128], P('layer', 'dp')
- bias_grad: float32 [6, 128], P('layer', 'dp')
All inputs are finite; a program needn't handle non-finite values.
Results may differ from a plain program's by a relative error of at most 0.007.
Values sent between devices are 32-bit elements; how exact they have to be, the bound alone decides.
A program may use at most 64 MiB of HBM per device.

v0:
```python
import functools

import jax
import jax.numpy as jnp
from jax import lax
from jax.experimental import pallas as pl
from jax.experimental.pallas import tpu as pltpu
from jax.sharding import PartitionSpec as P

MESH = pl.DeviceIdType.MESH
step_size = 0.5


def round_up(value, multiple):
    return -(-value // multiple) * multiple


def kernel(
    sections, peers, scale,
    states, weights, bias, guesses, gain,
    starts, weight_grad, bias_grad,
    x_in, w_in, g_in, wf, wt, x3, xt, slope, s3, adj, corr, msg, got, wacc, bacc,
    g, r1, h, r2, k, r3,
    w_sem, x_sem, g_sem, o_sem, m_send, m_recv,
    send1, recv1, send2, recv2, send3, recv3,
):
    depth, images, pairs, _, width, ch = states.shape
    depths = peers // 4
    block = weight_grad.shape[1]
    padded = round_up(block, 8)
    section = lax.axis_index("layer")
    me = lax.axis_index("dp")
    core = lax.rem(me, 2)
    col = lax.rem(lax.div(me, 2), 2)
    row = lax.div(me, 4)
    is_last = section == sections - 1
    not_last = section < sections - 1
    sends_on = section > 0

    def peer(row_at, col_at, core_at):
        return {"dp": (row_at * 2 + col_at) * 2 + core_at}

    around = [peer(row, col, 1 - core), peer(row, 1 - col, core)]
    around += [peer(lax.rem(row + hop, depths), col, core) for hop in range(1, depths)]

    barrier = pltpu.get_barrier_semaphore()
    for target in around:
        pl.semaphore_signal(barrier, inc=1, device_id=target, device_id_type=MESH)

    @pl.when(sends_on)
    def _():
        pl.semaphore_signal(barrier, inc=1, device_id={"layer": section - 1}, device_id_type=MESH)

    @pl.when(not_last)
    def _():
        pl.semaphore_signal(barrier, inc=1, device_id={"layer": section + 1}, device_id_type=MESH)

    def load_w(l):
        return pltpu.make_async_copy(weights.at[l], w_in.at[l], w_sem.at[l])

    def load_x(l, i):
        return pltpu.make_async_copy(states.at[l, i], x_in.at[l, i], x_sem.at[l, i])

    def load_g(i):
        return pltpu.make_async_copy(guesses.at[0, i], g_in.at[i], g_sem.at[i])

    for l in reversed(range(depth)):
        load_w(l).start()
        load_x(l, 0).start()
        if l == depth - 1:
            load_g(0).start()
    for i in range(1, images):
        for l in reversed(range(depth)):
            load_x(l, i).start()
        load_g(i).start()

    edge = jnp.zeros((width, 3 * ch), jnp.bfloat16)
    for l in range(depth):
        for i in range(images):
            for field in (x3, s3):
                field[l, i, 0, 0] = edge
                field[l, i, pairs, 1] = edge

    @pl.when(is_last)
    def _():
        corr[...] = jnp.zeros_like(corr)

    bacc[...] = jnp.zeros_like(bacc)

    @pl.loop(0, depth)
    def _(t):
        l = depth - 1 - t
        load_w(l).wait()
        wf[l, 0 : 9 * ch, 0:ch] = w_in[l]
        wf[l, 9 * ch : 12 * ch, 0:ch] = jnp.zeros((3 * ch, ch), jnp.bfloat16)
        wf[l, 0 : 3 * ch, ch : 2 * ch] = jnp.zeros((3 * ch, ch), jnp.bfloat16)
        wf[l, 3 * ch : 12 * ch, ch : 2 * ch] = w_in[l]
        for j in range(2):
            for r in range(4):
                for dx in range(3):
                    at = (r * 3 + dx) * ch
                    tap = (2 - (r - j)) * 3 + (2 - dx)
                    if 0 <= r - j <= 2:
                        part = w_in[l, tap * ch : (tap + 1) * ch, :]
                    else:
                        part = jnp.zeros((ch, ch), jnp.bfloat16)
                    wt[l, j * ch : (j + 1) * ch, at : at + ch] = part

    column = lax.broadcasted_iota(jnp.int32, (pairs, width, ch), 1)

    def spread(field, l, i, j, value):
        left = jnp.where(column == 0, 0.0, pltpu.roll(value, 1, 1))
        right = jnp.where(column == width - 1, 0.0, pltpu.roll(value, width - 1, 1))
        at = pl.ds(j, pairs)
        field[l, i, at, 1 - j, :, 0:ch] = left.astype(jnp.bfloat16)
        field[l, i, at, 1 - j, :, ch : 2 * ch] = value.astype(jnp.bfloat16)
        field[l, i, at, 1 - j, :, 2 * ch : 3 * ch] = right.astype(jnp.bfloat16)

    def windows(field, l, i):
        parts = [field[l, i, pl.ds(r // 2, pairs), r % 2] for r in range(4)]
        return jnp.concatenate(parts, axis=-1).reshape(pairs * width, 12 * ch)

    def slope_step(l, i):
        for j in range(2):
            spread(x3, l, i, j, x_in[l, i, :, j].astype(jnp.float32))
        out = lax.dot_general(
            windows(x3, l, i), wf[l], (((1,), (0,)), ((), ())), preferred_element_type=jnp.float32
        )
        offset = bias[pl.ds(l, 1), :]
        for j in range(2):
            value = jnp.tanh(out[:, j * ch : (j + 1) * ch] + offset)
            slope[l, i, :, j] = (1.0 - value * value).reshape(pairs, width, ch)

    def scale_step(l, i):
        for j in range(2):
            scaled = (slope[l, i, :, j] * adj[i, :, j]).astype(jnp.bfloat16).astype(jnp.float32)
            spread(s3, l, i, j, scaled)

    def adjoint_step(l, i):
        out = lax.dot_general(
            windows(s3, l, i), wt[l], (((1,), (1,)), ((), ())), preferred_element_type=jnp.float32
        )
        for j in range(2):
            part = out[:, j * ch : (j + 1) * ch].reshape(pairs, width, ch)
            adj[i, :, j] = adj[i, :, j] + step_size * part

    def turn_step(l, i):
        flat = [x3[l, i, pl.ds(j, pairs), 1 - j].reshape(pairs * width, 3 * ch) for j in range(2)]
        for j in range(2):
            xt[l, i, :, j * pairs * width : (j + 1) * pairs * width] = flat[j].T

    def grad_step(l, i, first):
        rows = []
        for j in range(2):
            parts = []
            for dy in range(3):
                r = j + 2 - dy
                parts.append(s3[l, i, pl.ds(r // 2, pairs), r % 2, :, ch : 2 * ch])
            rows.append(jnp.concatenate(parts, axis=-1).reshape(pairs * width, 3 * ch))
        right = jnp.concatenate(rows, axis=0)
        out = lax.dot_general(
            xt[l, i], right, (((1,), (0,)), ((), ())), preferred_element_type=jnp.float32
        )
        total = jnp.sum(right[:, ch : 2 * ch].astype(jnp.float32), axis=0, keepdims=True)
        bacc[pl.ds(l, 1), :] = bacc[pl.ds(l, 1), :] + total
        for dy in range(3):
            at = slice(dy * 3 * ch, (dy + 1) * 3 * ch)
            part = out[:, dy * ch : (dy + 1) * ch]
            wacc[l, at, :] = part if first else wacc[l, at, :] + part

    def message(i):
        return pltpu.make_async_remote_copy(
            src_ref=msg.at[i],
            dst_ref=got.at[i],
            send_sem=m_send.at[i],
            recv_sem=m_recv.at[i],
            device_id={"layer": section - 1},
            device_id_type=MESH,
        )

    def height(l):
        return padded if l else g.shape[4]

    def swap_cores(l):
        return pltpu.make_async_remote_copy(
            src_ref=g.at[l, 1 - core, :, :, 0 : height(l)],
            dst_ref=r1.at[l, :, :, 0 : height(l)],
            send_sem=send1.at[l],
            recv_sem=recv1.at[l],
            device_id=around[0],
            device_id_type=MESH,
        )

    def swap_cols(l):
        return pltpu.make_async_remote_copy(
            src_ref=h.at[l, 1 - col, :, 0 : height(l)],
            dst_ref=r2.at[l, :, 0 : height(l)],
            send_sem=send2.at[l],
            recv_sem=recv2.at[l],
            device_id=around[1],
            device_id_type=MESH,
        )

    def swap_rows(l, hop):
        return pltpu.make_async_remote_copy(
            src_ref=k.at[l, lax.rem(row + hop, depths), 0 : height(l)],
            dst_ref=r3.at[l, hop - 1, 0 : height(l)],
            send_sem=send3.at[l, hop - 1],
            recv_sem=recv3.at[l, hop - 1],
            device_id=around[1 + hop],
            device_id_type=MESH,
        )

    def reduce_1(l):
        for d in range(peers):
            at = (l, d % 2, (d // 2) % 2, d // 4)
            g[at + (slice(0, block),)] = wacc[l, d * block : (d + 1) * block, :]
            if l == 0:
                g[at + (slice(padded, None),)] = bacc[...]
        swap_cores(l).start()

    def reduce_2(l):
        n = height(l)
        swap_cores(l).wait_recv()
        h[l, 1 - col, :, 0:n] = g[l, core, 1 - col, :, 0:n] + r1[l, 1 - col, :, 0:n]
        swap_cols(l).start()
        h[l, col, :, 0:n] = g[l, core, col, :, 0:n] + r1[l, col, :, 0:n]

    def reduce_3(l):
        n = height(l)
        swap_cols(l).wait_recv()
        k[l, :, 0:n] = h[l, col, :, 0:n] + r2[l, :, 0:n]
        for hop in range(1, depths):
            swap_rows(l, hop).start()

    def reduce_4(l):
        n = height(l)
        total = k[l, row, 0:n]
        for hop in range(1, depths):
            swap_rows(l, hop).wait_recv()
            total = total + r3[l, hop - 1, 0:n]
        weight_grad[l] = scale * total[0:block]
        if l == 0:
            sums = total[padded : padded + depth]
            lane = lax.broadcasted_iota(jnp.int32, sums.shape, 1)
            share = bias_grad.shape[1]
            for at in range(share):
                mine = jnp.where(lane == me * share + at, sums, 0.0)
                bias_grad[:, at : at + 1] = scale * jnp.sum(mine, axis=1, keepdims=True)

    neighbours = sends_on.astype(jnp.int32) + not_last.astype(jnp.int32)
    pl.semaphore_wait(barrier, len(around) + neighbours)

    @pl.when(sends_on)
    def _():
        @pl.loop(0, images)
        def _(i):
            load_g(i).wait()
            adj[i] = g_in[i]

            @pl.loop(0, depth)
            def _(t):
                l = depth - 1 - t
                load_x(l, i).wait()
                slope_step(l, i)
                scale_step(l, i)
                adjoint_step(l, i)

            @pl.when(not_last)
            def _():
                message(i).wait_recv()
                corr[i] = got[i] - g_in[i]

            factor = gain[pl.ds(section - 1, 1), :].reshape(1, 1, 1, ch)
            msg[i] = adj[i] + factor * corr[i]
            message(i).start()

    @pl.when(jnp.logical_not(sends_on))
    def _():
        @pl.loop(0, images)
        def _(i):
            load_g(i).wait()

            @pl.loop(0, depth)
            def _(t):
                l = depth - 1 - t
                load_x(l, i).wait()
                slope_step(l, i)

    @pl.loop(0, images)
    def _(i):
        @pl.loop(0, depth)
        def _(l):
            turn_step(l, i)

    def begin(i):
        @pl.when(section == 0)
        def _():
            message(i).wait_recv()

        @pl.when(not_last)
        def _():
            adj[i] = got[i]

    def store(i):
        return pltpu.make_async_copy(adj.at[i], starts.at[0, i], o_sem.at[i])

    for i in range(images - 1):
        begin(i)

        @pl.loop(0, depth)
        def _(t):
            l = depth - 1 - t

            @pl.when(not_last)
            def _():
                scale_step(l, i)
                adjoint_step(l, i)

            grad_step(l, i, i == 0)

        store(i).start()

    i = images - 1
    begin(i)
    for l in reversed(range(depth)):
        @pl.when(not_last)
        def _():
            scale_step(l, i)

        grad_step(l, i, i == 0)
        reduce_1(l)

        @pl.when(not_last)
        def _():
            adjoint_step(l, i)

        reduce_2(l)
        if l < depth - 1:
            reduce_3(l + 1)
    store(i).start()
    reduce_3(0)
    for l in reversed(range(depth)):
        reduce_4(l)

    for i in range(images):
        store(i).wait()

        @pl.when(sends_on)
        def _():
            message(i).wait_send()

    for l in range(depth):
        swap_cores(l).wait_send()
        swap_cols(l).wait_send()
        for hop in range(1, depths):
            swap_rows(l, hop).wait_send()


def per_device(sections, peers, states, weights, bias, guesses, coarse_gain):
    depth, images, high, width, ch = states.shape
    pairs = high // 2
    rows = 9 * ch // peers
    depths = peers // 4
    tall = round_up(rows, 8) + round_up(depth, 8)
    scale = step_size / (images * peers)
    f32, bf16 = jnp.float32, jnp.bfloat16
    image = (images, pairs, 2, width, ch)
    taps = (depth, images, pairs + 1, 2, width, 3 * ch)
    dma = pltpu.SemaphoreType.DMA
    conv_flops = 2 * images * high * width * 9 * ch * ch
    vmem, anywhere = pl.BlockSpec(memory_space=pltpu.VMEM), pl.BlockSpec(memory_space=pl.ANY)
    starts, weight_grad, bias_grad = pl.pallas_call(
        functools.partial(kernel, sections, peers, scale),
        out_shape=(
            jax.ShapeDtypeStruct((1,) + image, f32),
            jax.ShapeDtypeStruct((depth, rows, ch), f32),
            jax.ShapeDtypeStruct((depth, ch // peers), f32),
        ),
        in_specs=[anywhere, anywhere, vmem, anywhere, vmem],
        out_specs=(anywhere, vmem, vmem),
        scratch_shapes=[
            pltpu.VMEM((depth,) + image, bf16),
            pltpu.VMEM((depth, 9 * ch, ch), bf16),
            pltpu.VMEM(image, f32),
            pltpu.VMEM((depth, 12 * ch, 2 * ch), bf16),
            pltpu.VMEM((depth, 2 * ch, 12 * ch), bf16),
            pltpu.VMEM(taps, bf16),
            pltpu.VMEM((depth, images, 3 * ch, high * width), bf16),
            pltpu.VMEM((depth,) + image, f32),
            pltpu.VMEM(taps, bf16),
            pltpu.VMEM(image, f32),
            pltpu.VMEM(image, f32),
            pltpu.VMEM(image, f32),
            pltpu.VMEM(image, f32),
            pltpu.VMEM((depth, 9 * ch, ch), f32),
            pltpu.VMEM((round_up(depth, 8), ch), f32),
            pltpu.VMEM((depth, 2, 2, depths, tall, ch), f32),
            pltpu.VMEM((depth, 2, depths, tall, ch), f32),
            pltpu.VMEM((depth, 2, depths, tall, ch), f32),
            pltpu.VMEM((depth, depths, tall, ch), f32),
            pltpu.VMEM((depth, depths, tall, ch), f32),
            pltpu.VMEM((depth, depths, tall, ch), f32),
            dma((depth,)), dma((depth, images)), dma((images,)), dma((images,)),
            dma((images,)), dma((images,)),
            dma((depth,)), dma((depth,)), dma((depth,)), dma((depth,)),
            dma((depth, depths)), dma((depth, depths)),
        ],
        compiler_params=pltpu.CompilerParams(
            collective_id=0, has_side_effects=True, vmem_limit_bytes=56 * 1024 * 1024
        ),
        cost_estimate=pl.CostEstimate(
            flops=9 * conv_flops, bytes_accessed=8 * states.size, transcendentals=states.size
        ),
    )(
        states.reshape((depth,) + image),
        weights,
        bias,
        guesses.reshape((1,) + image),
        coarse_gain,
    )
    return starts.reshape(guesses.shape), weight_grad, bias_grad


def solution(mesh):
    return jax.shard_map(
        functools.partial(per_device, mesh.shape["layer"], mesh.shape["dp"]),
        mesh=mesh,
        in_specs=(
            P("layer", "dp", None, None, None),
            P("layer", None, None),
            P("layer", None),
            P("layer", "dp", None, None, None),
            P(),
        ),
        out_specs=(P("layer", "dp", None, None, None), P("layer", "dp", None), P("layer", "dp")),
        check_vma=False,
    )
```

profile of v0, /device:TPU:0, one launch (start us, length us, event | category | flops | bytes accessed | tf_op | source)
XLA Modules:
  0.0 60.6 jit_solution(8641802534952882951)
XLA Ops:
  0.6 56.5 %shard_map.76 = (f32[1,2,16,2,32,128]{5,4,3,2,1,0:T(8,128)}, f32[3,72,128]{2,1,0:T(8,128)}, f32[3,8]{1,0:T(4,128)}) custom-call(bf16[3,2,16,2,32,128]{5,4,3,2,1,0:T(8,128)(2,1)} %bitcast.4, bf16[3,1152,128]{2,1,0:T(8,128)(2,1)} %weights.1, f32[3,128]{1,0:T(4,128)} %bias.1, f32[1,2,16,2,32,128]{5,4,3,2,1,0:T(8,128)} %bitcast.5, f32[2,128]{1,0:T(2,128)} %gain.1), custom_call_target="tpu_custom_call" | custom-call | flops 5435817984 | bytes 6291456 | tf_op jit(solution)/shard_map/pallas_call | solution.py:373
  57.1 0.0 copy-start
  57.1 0.0 copy-start.1
  57.1 2.3 %copy.11 = f32[1,2,32,32,128]{4,3,2,1,0:T(8,128)} copy(f32[1,2,32,32,128]{4,3,2,1,0:T(8,128)} %bitcast.3) | data formatting | bytes 2097152
  59.4 0.0 copy-done
  59.4 0.6 %copy.12 = f32[3,72,128]{2,1,0:T(8,128)} copy(f32[3,72,128]{2,1,0:T(8,128)S(1)} %copy-done) | data formatting | bytes 221184
  60.1 0.0 copy-done.1
  60.1 0.6 copy.13
Async XLA Ops:
  57.1 2.3 %copy-start = (f32[3,72,128]{2,1,0:T(8,128)S(1)}, f32[3,72,128]{2,1,0:T(8,128)}, u32[]{:S(2)}) copy-start(f32[3,72,128]{2,1,0:T(8,128)} %get-tuple-element.13) | copy-start | bytes 331780
  57.1 3.0 %copy-start.1 = (f32[3,8]{1,0:T(4,128)S(1)}, f32[3,8]{1,0:T(4,128)}, u32[]{:S(2)}) copy-start(f32[3,8]{1,0:T(4,128)} %get-tuple-element.14) | copy-start | bytes 292
where the time goes:
time: 60.8 us; the launch traced here: 60.6 us
  Pallas kernels  56.5 us (93%)
  local copies, waits for them, and re-layouts  3.53 us (6%)
  between operations  0.66 us (1%)
    pallas_call x1, Pallas kernels, per_device(): pl.pallas_call(functools.partial(kernel, sections, peers, scale), out_sha...  56.5 us
    unnamed x7, local copies, waits for them, and re-layouts  3.53 us

commit v1 on v0

--- a/solution.py
+++ b/solution.py
@@ -95,23 +95,24 @@
         wf[l, 9 * ch : 12 * ch, 0:ch] = jnp.zeros((3 * ch, ch), jnp.bfloat16)
         wf[l, 0 : 3 * ch, ch : 2 * ch] = jnp.zeros((3 * ch, ch), jnp.bfloat16)
         wf[l, 3 * ch : 12 * ch, ch : 2 * ch] = w_in[l]
-        for j in range(2):
-            for r in range(4):
-                for dx in range(3):
-                    at = (r * 3 + dx) * ch
-                    tap = (2 - (r - j)) * 3 + (2 - dx)
-                    if 0 <= r - j <= 2:
-                        part = w_in[l, tap * ch : (tap + 1) * ch, :]
-                    else:
-                        part = jnp.zeros((ch, ch), jnp.bfloat16)
-                    wt[l, j * ch : (j + 1) * ch, at : at + ch] = part
-
-    column = lax.broadcasted_iota(jnp.int32, (pairs, width, ch), 1)
-
-    def spread(field, l, i, j, value):
-        left = jnp.where(column == 0, 0.0, pltpu.roll(value, 1, 1))
-        right = jnp.where(column == width - 1, 0.0, pltpu.roll(value, width - 1, 1))
-        at = pl.ds(j, pairs)
+        for tap in range(9):
+            turned = w_in[l, tap * ch : (tap + 1) * ch, :].T
+            dy, dx = 2 - tap // 3, 2 - tap % 3
+            for j in range(2):
+                at = ((dy + j) * 3 + dx) * ch
+                wt[l, at : at + ch, j * ch : (j + 1) * ch] = turned
+        wt[l, 9 * ch : 12 * ch, 0:ch] = jnp.zeros((3 * ch, ch), jnp.bfloat16)
+        wt[l, 0 : 3 * ch, ch : 2 * ch] = jnp.zeros((3 * ch, ch), jnp.bfloat16)
+
+    column = lax.broadcasted_iota(jnp.int32, (1, width, ch), 1)
+    leftmost, rightmost = column == 0, column == width - 1
+    chunk = 4
+    chunks = [slice(q, q + chunk) for q in range(0, pairs, chunk)]
+
+    def spread(field, l, i, j, q, value):
+        left = jnp.where(leftmost, 0.0, pltpu.roll(value, 1, 1))
+        right = jnp.where(rightmost, 0.0, pltpu.roll(value, width - 1, 1))
+        at = slice(q.start + j, q.stop + j)
         field[l, i, at, 1 - j, :, 0:ch] = left.astype(jnp.bfloat16)
         field[l, i, at, 1 - j, :, ch : 2 * ch] = value.astype(jnp.bfloat16)
         field[l, i, at, 1 - j, :, 2 * ch : 3 * ch] = right.astype(jnp.bfloat16)
@@ -121,28 +122,32 @@
         return jnp.concatenate(parts, axis=-1).reshape(pairs * width, 12 * ch)
 
     def slope_step(l, i):
-        for j in range(2):
-            spread(x3, l, i, j, x_in[l, i, :, j].astype(jnp.float32))
+        for q in chunks:
+            for j in range(2):
+                spread(x3, l, i, j, q, x_in[l, i, q, j].astype(jnp.float32))
         out = lax.dot_general(
             windows(x3, l, i), wf[l], (((1,), (0,)), ((), ())), preferred_element_type=jnp.float32
         )
         offset = bias[pl.ds(l, 1), :]
-        for j in range(2):
-            value = jnp.tanh(out[:, j * ch : (j + 1) * ch] + offset)
-            slope[l, i, :, j] = (1.0 - value * value).reshape(pairs, width, ch)
+        for q in chunks:
+            for j in range(2):
+                part = out[q.start * width : q.stop * width, j * ch : (j + 1) * ch]
+                value = jnp.tanh(part + offset)
+                slope[l, i, q, j] = (1.0 - value * value).reshape(chunk, width, ch)
 
     def scale_step(l, i):
-        for j in range(2):
-            scaled = (slope[l, i, :, j] * adj[i, :, j]).astype(jnp.bfloat16).astype(jnp.float32)
-            spread(s3, l, i, j, scaled)
+        for q in chunks:
+            for j in range(2):
+                spread(s3, l, i, j, q, slope[l, i, q, j] * adj[i, q, j])
 
     def adjoint_step(l, i):
         out = lax.dot_general(
-            windows(s3, l, i), wt[l], (((1,), (1,)), ((), ())), preferred_element_type=jnp.float32
-        )
-        for j in range(2):
-            part = out[:, j * ch : (j + 1) * ch].reshape(pairs, width, ch)
-            adj[i, :, j] = adj[i, :, j] + step_size * part
+            windows(s3, l, i), wt[l], (((1,), (0,)), ((), ())), preferred_element_type=jnp.float32
+        )
+        for q in chunks:
+            for j in range(2):
+                part = out[q.start * width : q.stop * width, j * ch : (j + 1) * ch]
+                adj[i, q, j] = adj[i, q, j] + step_size * part.reshape(chunk, width, ch)
 
     def turn_step(l, i):
         flat = [x3[l, i, pl.ds(j, pairs), 1 - j].reshape(pairs * width, 3 * ch) for j in range(2)]
@@ -355,6 +360,21 @@
         swap_cols(l).wait_send()
         for hop in range(1, depths):
             swap_rows(l, hop).wait_send()
+
+
+def hand_over(parts, starts, weight_grad, bias_grad, starts_out, weight_out, bias_out, sem):
+    per_image = parts // starts.shape[1]
+    some = starts.shape[2] // per_image
+    copies = []
+    for part in range(parts):
+        at = (0, part // per_image, pl.ds(part % per_image * some, some))
+        copies.append(pltpu.make_async_copy(starts.at[at], starts_out.at[at], sem.at[part]))
+    copies.append(pltpu.make_async_copy(weight_grad, weight_out, sem.at[parts]))
+    copies.append(pltpu.make_async_copy(bias_grad, bias_out, sem.at[parts + 1]))
+    for copy in copies:
+        copy.start()
+    for copy in copies:
+        copy.wait()
 
 
 def per_device(sections, peers, states, weights, bias, guesses, coarse_gain):
@@ -384,7 +404,7 @@
             pltpu.VMEM((depth, 9 * ch, ch), bf16),
             pltpu.VMEM(image, f32),
             pltpu.VMEM((depth, 12 * ch, 2 * ch), bf16),
-            pltpu.VMEM((depth, 2 * ch, 12 * ch), bf16),
+            pltpu.VMEM((depth, 12 * ch, 2 * ch), bf16),
             pltpu.VMEM(taps, bf16),
             pltpu.VMEM((depth, images, 3 * ch, high * width), bf16),
             pltpu.VMEM((depth,) + image, f32),
@@ -419,6 +439,19 @@
         guesses.reshape((1,) + image),
         coarse_gain,
     )
+    parts = images * 4
+    starts, weight_grad, bias_grad = pl.pallas_call(
+        functools.partial(hand_over, parts),
+        out_shape=(
+            jax.ShapeDtypeStruct(starts.shape, f32),
+            jax.ShapeDtypeStruct(weight_grad.shape, f32),
+            jax.ShapeDtypeStruct(bias_grad.shape, f32),
+        ),
+        in_specs=[anywhere] * 3,
+        out_specs=(anywhere,) * 3,
+        scratch_shapes=[dma((parts + 2,))],
+        compiler_params=pltpu.CompilerParams(vmem_limit_bytes=56 * 1024 * 1024),
+    )(starts, weight_grad, bias_grad)
     return starts.reshape(guesses.shape), weight_grad, bias_grad
 
 

time: 60.8 us -> 93.5 us (1.54)
  Pallas kernels: 56.5 us -> 92.7 us
  local copies, waits for them, and re-layouts: 3.53 us -> 0 us
    pallas_call x0 -> x1, Pallas kernels: none -> 36.4 us  [per_device(): pl.pallas_call(functools.partial(hand_over, parts), out_shape=(jax.ShapeD...]
    unnamed x7 -> x0, local copies, waits for them, and re-layouts: 3.53 us -> none
where the time goes in v1:
time: 93.5 us; the launch traced here: 93.3 us
  Pallas kernels  92.7 us (99%)
    pallas_call x1, Pallas kernels, per_device(): pl.pallas_call(functools.partial(kernel, sections, peers, scale), out_sha...  56.3 us
    pallas_call x1, Pallas kernels, per_device(): pl.pallas_call(functools.partial(hand_over, parts), out_shape=(jax.ShapeD...  36.4 us

profile of v1, /device:TPU:0, one launch (start us, length us, event | category | flops | bytes accessed | tf_op | source)
XLA Modules:
  0.0 93.3 jit_solution(1463063914300885846)
XLA Ops:
  0.6 56.3 %shard_map.76 = (f32[1,2,16,2,32,128]{5,4,3,2,1,0:T(8,128)}, f32[3,72,128]{2,1,0:T(8,128)}, f32[3,8]{1,0:T(4,128)}) custom-call(bf16[3,2,16,2,32,128]{5,4,3,2,1,0:T(8,128)(2,1)} %bitcast.3, bf16[3,1152,128]{2,1,0:T(8,128)(2,1)} %weights.1, f32[3,128]{1,0:T(4,128)} %bias.1, f32[1,2,16,2,32,128]{5,4,3,2,1,0:T(8,128)} %bitcast.4, f32[2,128]{1,0:T(2,128)} %gain.1), custom_call_target="tpu_custom_call" | custom-call | flops 5435817984 | bytes 6291456 | tf_op jit(solution)/shard_map/pallas_call | solution.py:393
  57.0 36.4 %shard_map.77 = (f32[1,2,16,2,32,128]{5,4,3,2,1,0:T(8,128)}, f32[3,72,128]{2,1,0:T(8,128)}, f32[3,8]{1,0:T(4,128)}) custom-call(f32[1,2,16,2,32,128]{5,4,3,2,1,0:T(8,128)} %get-tuple-element.9.starts, f32[3,72,128]{2,1,0:T(8,128)} %get-tuple-element.10.weight_grad, f32[3,8]{1,0:T(4,128)} %get-tuple-element.11.bias_grad), custom_call_target="tpu_custom_call" | custom-call | tf_op jit(solution)/shard_map/pallas_call | solution.py:443

commit v2 on v1

--- a/solution.py
+++ b/solution.py
@@ -173,15 +173,34 @@
             part = out[:, dy * ch : (dy + 1) * ch]
             wacc[l, at, :] = part if first else wacc[l, at, :] + part
 
-    def message(i):
-        return pltpu.make_async_remote_copy(
-            src_ref=msg.at[i],
-            dst_ref=got.at[i],
-            send_sem=m_send.at[i],
-            recv_sem=m_recv.at[i],
-            device_id={"layer": section - 1},
-            device_id_type=MESH,
-        )
+    pieces = 4
+    piece = pairs // pieces
+
+    class message:
+        def __init__(self, i):
+            self.copies = [
+                pltpu.make_async_remote_copy(
+                    src_ref=msg.at[i, pl.ds(at * piece, piece)],
+                    dst_ref=got.at[i, pl.ds(at * piece, piece)],
+                    send_sem=m_send.at[i, at],
+                    recv_sem=m_recv.at[i, at],
+                    device_id={"layer": section - 1},
+                    device_id_type=MESH,
+                )
+                for at in range(pieces)
+            ]
+
+        def start(self):
+            for copy in self.copies:
+                copy.start()
+
+        def wait_recv(self):
+            for copy in self.copies:
+                copy.wait_recv()
+
+        def wait_send(self):
+            for copy in self.copies:
+                copy.wait_send()
 
     def height(l):
         return padded if l else g.shape[4]
@@ -362,19 +381,25 @@
             swap_rows(l, hop).wait_send()
 
 
-def hand_over(parts, starts, weight_grad, bias_grad, starts_out, weight_out, bias_out, sem):
-    per_image = parts // starts.shape[1]
-    some = starts.shape[2] // per_image
-    copies = []
-    for part in range(parts):
-        at = (0, part // per_image, pl.ds(part % per_image * some, some))
-        copies.append(pltpu.make_async_copy(starts.at[at], starts_out.at[at], sem.at[part]))
-    copies.append(pltpu.make_async_copy(weight_grad, weight_out, sem.at[parts]))
-    copies.append(pltpu.make_async_copy(bias_grad, bias_out, sem.at[parts + 1]))
-    for copy in copies:
-        copy.start()
-    for copy in copies:
-        copy.wait()
+def hand_over(starts, weight_grad, bias_grad, starts_out, weight_out, bias_out, held, in_sem, out_sem):
+    images, pairs = starts.shape[1:3]
+    parts = 4 if pairs % 4 == 0 else 1
+    some = pairs // parts
+    loads, stores = [], []
+    for i in range(images):
+        for part in range(parts):
+            at, n = (0, i, pl.ds(part * some, some)), i * parts + part
+            loads.append(pltpu.make_async_copy(starts.at[at], held.at[at], in_sem.at[n]))
+            stores.append(pltpu.make_async_copy(held.at[at], starts_out.at[at], out_sem.at[n]))
+    for load in loads:
+        load.start()
+    weight_out[...] = weight_grad[...]
+    bias_out[...] = bias_grad[...]
+    for load, store in zip(loads, stores):
+        load.wait()
+        store.start()
+    for store in stores:
+        store.wait()
 
 
 def per_device(sections, peers, states, weights, bias, guesses, coarse_gain):
@@ -422,7 +447,7 @@
             pltpu.VMEM((depth, depths, tall, ch), f32),
             pltpu.VMEM((depth, depths, tall, ch), f32),
             dma((depth,)), dma((depth, images)), dma((images,)), dma((images,)),
-            dma((images,)), dma((images,)),
+            dma((images, 4)), dma((images, 4)),
             dma((depth,)), dma((depth,)), dma((depth,)), dma((depth,)),
             dma((depth, depths)), dma((depth, depths)),
         ],
@@ -439,18 +464,17 @@
         guesses.reshape((1,) + image),
         coarse_gain,
     )
-    parts = images * 4
     starts, weight_grad, bias_grad = pl.pallas_call(
-        functools.partial(hand_over, parts),
+        hand_over,
         out_shape=(
             jax.ShapeDtypeStruct(starts.shape, f32),
             jax.ShapeDtypeStruct(weight_grad.shape, f32),
             jax.ShapeDtypeStruct(bias_grad.shape, f32),
         ),
-        in_specs=[anywhere] * 3,
-        out_specs=(anywhere,) * 3,
-        scratch_shapes=[dma((parts + 2,))],
-        compiler_params=pltpu.CompilerParams(vmem_limit_bytes=56 * 1024 * 1024),
+        in_specs=[anywhere, vmem, vmem],
+        out_specs=(anywhere, vmem, vmem),
+        scratch_shapes=[pltpu.VMEM(starts.shape, f32), dma((images * 4,)), dma((images * 4,))],
+        compiler_params=pltpu.CompilerParams(vmem_limit_bytes=60 * 1024 * 1024),
     )(starts, weight_grad, bias_grad)
     return starts.reshape(guesses.shape), weight_grad, bias_grad
 

time: 93.5 us -> 60.9 us (0.65)
  Pallas kernels: 92.7 us -> 60.1 us
    pallas_call x1, Pallas kernels: 36.4 us -> 3.63 us  [per_device(): pl.pallas_call(hand_over, out_shape=(jax.ShapeDtypeStruct(starts.shape, f...]
where the time goes in v2:
time: 60.9 us; the launch traced here: 60.7 us
  Pallas kernels  60.1 us (99%)
  between operations  0.64 us (1%)
    pallas_call x1, Pallas kernels, per_device(): pl.pallas_call(functools.partial(kernel, sections, peers, scale), out_sha...  56.4 us
    pallas_call x1, Pallas kernels, per_device(): pl.pallas_call(hand_over, out_shape=(jax.ShapeDtypeStruct(starts.shape, f...  3.63 us

profile of v2, /device:TPU:0, one launch (start us, length us, event | category | flops | bytes accessed | tf_op | source)
XLA Modules:
  0.0 60.7 jit_solution(6161668019187482475)
XLA Ops:
  0.6 56.4 %shard_map.76 = (f32[1,2,16,2,32,128]{5,4,3,2,1,0:T(8,128)}, f32[3,72,128]{2,1,0:T(8,128)}, f32[3,8]{1,0:T(4,128)}) custom-call(bf16[3,2,16,2,32,128]{5,4,3,2,1,0:T(8,128)(2,1)} %bitcast.3, bf16[3,1152,128]{2,1,0:T(8,128)(2,1)} %weights.1, f32[3,128]{1,0:T(4,128)} %bias.1, f32[1,2,16,2,32,128]{5,4,3,2,1,0:T(8,128)} %bitcast.4, f32[2,128]{1,0:T(2,128)} %gain.1), custom_call_target="tpu_custom_call" | custom-call | flops 5435817984 | bytes 6291456 | tf_op jit(solution)/shard_map/pallas_call | solution.py:418
  57.1 3.6 %shard_map.77 = (f32[1,2,16,2,32,128]{5,4,3,2,1,0:T(8,128)}, f32[3,72,128]{2,1,0:T(8,128)}, f32[3,8]{1,0:T(4,128)}) custom-call(f32[1,2,16,2,32,128]{5,4,3,2,1,0:T(8,128)} %get-tuple-element.9.starts, f32[3,72,128]{2,1,0:T(8,128)} %get-tuple-element.10.weight_grad, f32[3,8]{1,0:T(4,128)} %get-tuple-element.11.bias_grad), custom_call_target="tpu_custom_call" | custom-call | tf_op jit(solution)/shard_map/pallas_call | solution.py:467

commit v3 on v2

--- a/solution.py
+++ b/solution.py
@@ -106,8 +106,9 @@
 
     column = lax.broadcasted_iota(jnp.int32, (1, width, ch), 1)
     leftmost, rightmost = column == 0, column == width - 1
-    chunk = 4
-    chunks = [slice(q, q + chunk) for q in range(0, pairs, chunk)]
+
+    def chunks(lo, hi):
+        return [slice(q, min(q + 4, hi)) for q in range(lo, hi, 4)]
 
     def spread(field, l, i, j, q, value):
         left = jnp.where(leftmost, 0.0, pltpu.roll(value, 1, 1))
@@ -117,37 +118,41 @@
         field[l, i, at, 1 - j, :, ch : 2 * ch] = value.astype(jnp.bfloat16)
         field[l, i, at, 1 - j, :, 2 * ch : 3 * ch] = right.astype(jnp.bfloat16)
 
-    def windows(field, l, i):
-        parts = [field[l, i, pl.ds(r // 2, pairs), r % 2] for r in range(4)]
-        return jnp.concatenate(parts, axis=-1).reshape(pairs * width, 12 * ch)
-
-    def slope_step(l, i):
-        for q in chunks:
+    def windows(field, l, i, lo, hi):
+        parts = [field[l, i, pl.ds(lo + r // 2, hi - lo), r % 2] for r in range(4)]
+        return jnp.concatenate(parts, axis=-1).reshape((hi - lo) * width, 12 * ch)
+
+    def product(field, kernels, l, i, lo, hi):
+        out = lax.dot_general(
+            windows(field, l, i, lo, hi),
+            kernels[l],
+            (((1,), (0,)), ((), ())),
+            preferred_element_type=jnp.float32,
+        )
+        for q in chunks(lo, hi):
+            for j in range(2):
+                at = slice((q.start - lo) * width, (q.stop - lo) * width)
+                yield q, j, out[at, j * ch : (j + 1) * ch].reshape(q.stop - q.start, width, ch)
+
+    def field_step(l, i, lo, hi):
+        for q in chunks(lo, hi):
             for j in range(2):
                 spread(x3, l, i, j, q, x_in[l, i, q, j].astype(jnp.float32))
-        out = lax.dot_general(
-            windows(x3, l, i), wf[l], (((1,), (0,)), ((), ())), preferred_element_type=jnp.float32
-        )
-        offset = bias[pl.ds(l, 1), :]
-        for q in chunks:
-            for j in range(2):
-                part = out[q.start * width : q.stop * width, j * ch : (j + 1) * ch]
-                value = jnp.tanh(part + offset)
-                slope[l, i, q, j] = (1.0 - value * value).reshape(chunk, width, ch)
-
-    def scale_step(l, i):
-        for q in chunks:
+
+    def slope_step(l, i, lo, hi):
+        offset = bias[pl.ds(l, 1), :].reshape(1, 1, ch)
+        for q, j, part in product(x3, wf, l, i, lo, hi):
+            value = jnp.tanh(part + offset)
+            slope[l, i, q, j] = 1.0 - value * value
+
+    def scale_step(l, i, lo, hi):
+        for q in chunks(lo, hi):
             for j in range(2):
                 spread(s3, l, i, j, q, slope[l, i, q, j] * adj[i, q, j])
 
-    def adjoint_step(l, i):
-        out = lax.dot_general(
-            windows(s3, l, i), wt[l], (((1,), (0,)), ((), ())), preferred_element_type=jnp.float32
-        )
-        for q in chunks:
-            for j in range(2):
-                part = out[q.start * width : q.stop * width, j * ch : (j + 1) * ch]
-                adj[i, q, j] = adj[i, q, j] + step_size * part.reshape(chunk, width, ch)
+    def adjoint_step(l, i, lo, hi):
+        for q, j, part in product(s3, wt, l, i, lo, hi):
+            adj[i, q, j] = adj[i, q, j] + step_size * part
 
     def turn_step(l, i):
         flat = [x3[l, i, pl.ds(j, pairs), 1 - j].reshape(pairs * width, 3 * ch) for j in range(2)]
@@ -176,61 +181,49 @@
     pieces = 4
     piece = pairs // pieces
 
-    class message:
-        def __init__(self, i):
-            self.copies = [
-                pltpu.make_async_remote_copy(
-                    src_ref=msg.at[i, pl.ds(at * piece, piece)],
-                    dst_ref=got.at[i, pl.ds(at * piece, piece)],
-                    send_sem=m_send.at[i, at],
-                    recv_sem=m_recv.at[i, at],
-                    device_id={"layer": section - 1},
-                    device_id_type=MESH,
-                )
-                for at in range(pieces)
-            ]
-
-        def start(self):
-            for copy in self.copies:
-                copy.start()
-
-        def wait_recv(self):
-            for copy in self.copies:
-                copy.wait_recv()
-
-        def wait_send(self):
-            for copy in self.copies:
-                copy.wait_send()
+    def message(i, at):
+        return pltpu.make_async_remote_copy(
+            src_ref=msg.at[i, pl.ds(at * piece, piece)],
+            dst_ref=got.at[i, pl.ds(at * piece, piece)],
+            send_sem=m_send.at[i, at],
+            recv_sem=m_recv.at[i, at],
+            device_id={"layer": section - 1},
+            device_id_type=MESH,
+        )
 
     def height(l):
         return padded if l else g.shape[4]
 
-    def swap_cores(l):
+    def span(l, part):
+        cut = round_up(padded // 2, 8)
+        return slice(cut, height(l)) if part else slice(0, cut)
+
+    def swap_cores(l, part):
         return pltpu.make_async_remote_copy(
-            src_ref=g.at[l, 1 - core, :, :, 0 : height(l)],
-            dst_ref=r1.at[l, :, :, 0 : height(l)],
-            send_sem=send1.at[l],
-            recv_sem=recv1.at[l],
+            src_ref=g.at[l, 1 - core, :, :, span(l, part)],
+            dst_ref=r1.at[l, :, :, span(l, part)],
+            send_sem=send1.at[l, part],
+            recv_sem=recv1.at[l, part],
             device_id=around[0],
             device_id_type=MESH,
         )
 
-    def swap_cols(l):
+    def swap_cols(l, part):
         return pltpu.make_async_remote_copy(
-            src_ref=h.at[l, 1 - col, :, 0 : height(l)],
-            dst_ref=r2.at[l, :, 0 : height(l)],
-            send_sem=send2.at[l],
-            recv_sem=recv2.at[l],
+            src_ref=h.at[l, 1 - col, :, span(l, part)],
+            dst_ref=r2.at[l, :, span(l, part)],
+            send_sem=send2.at[l, part],
+            recv_sem=recv2.at[l, part],
             device_id=around[1],
             device_id_type=MESH,
         )
 
-    def swap_rows(l, hop):
+    def swap_rows(l, part, hop):
         return pltpu.make_async_remote_copy(
-            src_ref=k.at[l, lax.rem(row + hop, depths), 0 : height(l)],
-            dst_ref=r3.at[l, hop - 1, 0 : height(l)],
-            send_sem=send3.at[l, hop - 1],
-            recv_sem=recv3.at[l, hop - 1],
+            src_ref=k.at[l, lax.rem(row + hop, depths), span(l, part)],
+            dst_ref=r3.at[l, hop - 1, span(l, part)],
+            send_sem=send3.at[l, part, hop - 1],
+            recv_sem=recv3.at[l, part, hop - 1],
             device_id=around[1 + hop],
             device_id_type=MESH,
         )
@@ -241,39 +234,71 @@
             g[at + (slice(0, block),)] = wacc[l, d * block : (d + 1) * block, :]
             if l == 0:
                 g[at + (slice(padded, None),)] = bacc[...]
-        swap_cores(l).start()
-
-    def reduce_2(l):
-        n = height(l)
-        swap_cores(l).wait_recv()
-        h[l, 1 - col, :, 0:n] = g[l, core, 1 - col, :, 0:n] + r1[l, 1 - col, :, 0:n]
-        swap_cols(l).start()
-        h[l, col, :, 0:n] = g[l, core, col, :, 0:n] + r1[l, col, :, 0:n]
-
-    def reduce_3(l):
-        n = height(l)
-        swap_cols(l).wait_recv()
-        k[l, :, 0:n] = h[l, col, :, 0:n] + r2[l, :, 0:n]
+        for part in range(2):
+            swap_cores(l, part).start()
+
+    def reduce_2(l, part):
+        n = span(l, part)
+        swap_cores(l, part).wait_recv()
+        h[l, 1 - col, :, n] = g[l, core, 1 - col, :, n] + r1[l, 1 - col, :, n]
+        swap_cols(l, part).start()
+        h[l, col, :, n] = g[l, core, col, :, n] + r1[l, col, :, n]
+
+    def reduce_3(l, part):
+        n = span(l, part)
+        swap_cols(l, part).wait_recv()
+        k[l, :, n] = h[l, col, :, n] + r2[l, :, n]
         for hop in range(1, depths):
-            swap_rows(l, hop).start()
-
-    def reduce_4(l):
-        n = height(l)
-        total = k[l, row, 0:n]
+            swap_rows(l, part, hop).start()
+
+    def reduce_4(l, part):
+        n = span(l, part)
+        total = k[l, row, n]
         for hop in range(1, depths):
-            swap_rows(l, hop).wait_recv()
-            total = total + r3[l, hop - 1, 0:n]
-        weight_grad[l] = scale * total[0:block]
-        if l == 0:
-            sums = total[padded : padded + depth]
+            swap_rows(l, part, hop).wait_recv()
+            total = total + r3[l, hop - 1, n]
+        last = min(n.stop, block)
+        weight_grad[l, n.start : last] = scale * total[0 : last - n.start]
+        if l == 0 and part == 1:
+            sums = total[padded - n.start : padded - n.start + depth]
             lane = lax.broadcasted_iota(jnp.int32, sums.shape, 1)
             share = bias_grad.shape[1]
             for at in range(share):
                 mine = jnp.where(lane == me * share + at, sums, 0.0)
                 bias_grad[:, at : at + 1] = scale * jnp.sum(mine, axis=1, keepdims=True)
 
-    neighbours = sends_on.astype(jnp.int32) + not_last.astype(jnp.int32)
-    pl.semaphore_wait(barrier, len(around) + neighbours)
+    def all_here():
+        neighbours = sends_on.astype(jnp.int32) + not_last.astype(jnp.int32)
+        pl.semaphore_wait(barrier, len(around) + neighbours)
+
+    half = pairs // 2
+
+    def first_pass(i, band):
+        def part_of(extra):
+            cut = min(half + extra, pairs)
+            return (cut, pairs) if band else (0, cut)
+
+        for l in reversed(range(depth)):
+            if band == 0:
+                load_x(l, i).wait()
+            field_step(l, i, *part_of(l + 2))
+            slope_step(l, i, *part_of(l + 1))
+            scale_step(l, i, *part_of(l + 1))
+            adjoint_step(l, i, *part_of(l))
+
+    def send_band(i, band):
+        factor = gain[pl.ds(section - 1, 1), :].reshape(1, 1, 1, ch)
+        count = pieces // 2
+        for at in range(band * count, (band + 1) * count):
+            rows = slice(at * piece, (at + 1) * piece)
+
+            @pl.when(not_last)
+            def _():
+                message(i, at).wait_recv()
+                corr[i, rows] = got[i, rows] - g_in[i, rows]
+
+            msg[i, rows] = adj[i, rows] + factor * corr[i, rows]
+            message(i, at).start()
 
     @pl.when(sends_on)
     def _():
@@ -281,23 +306,15 @@
         def _(i):
             load_g(i).wait()
             adj[i] = g_in[i]
-
-            @pl.loop(0, depth)
-            def _(t):
-                l = depth - 1 - t
-                load_x(l, i).wait()
-                slope_step(l, i)
-                scale_step(l, i)
-                adjoint_step(l, i)
-
-            @pl.when(not_last)
+            first_pass(i, 0)
+
+            @pl.when(i == 0)
             def _():
-                message(i).wait_recv()
-                corr[i] = got[i] - g_in[i]
-
-            factor = gain[pl.ds(section - 1, 1), :].reshape(1, 1, 1, ch)
-            msg[i] = adj[i] + factor * corr[i]
-            message(i).start()
+                all_here()
+
+            send_band(i, 0)
+            first_pass(i, 1)
+            send_band(i, 1)
 
     @pl.when(jnp.logical_not(sends_on))
     def _():
@@ -309,7 +326,10 @@
             def _(t):
                 l = depth - 1 - t
                 load_x(l, i).wait()
-                slope_step(l, i)
+                field_step(l, i, 0, pairs)
+                slope_step(l, i, 0, pairs)
+
+        all_here()
 
     @pl.loop(0, images)
     def _(i):
@@ -320,7 +340,8 @@
     def begin(i):
         @pl.when(section == 0)
         def _():
-            message(i).wait_recv()
+            for at in range(pieces):
+                message(i, at).wait_recv()
 
         @pl.when(not_last)
         def _():
@@ -338,8 +359,8 @@
 
             @pl.when(not_last)
             def _():
-                scale_step(l, i)
-                adjoint_step(l, i)
+                scale_step(l, i, 0, pairs)
+                adjoint_step(l, i, 0, pairs)
 
             grad_step(l, i, i == 0)
 
@@ -350,51 +371,56 @@
     for l in reversed(range(depth)):
         @pl.when(not_last)
         def _():
-            scale_step(l, i)
+            scale_step(l, i, 0, pairs)
 
         grad_step(l, i, i == 0)
         reduce_1(l)
 
         @pl.when(not_last)
         def _():
-            adjoint_step(l, i)
-
-        reduce_2(l)
+            adjoint_step(l, i, 0, pairs)
+
+        for part in range(2):
+            reduce_2(l, part)
         if l < depth - 1:
-            reduce_3(l + 1)
+            for part in range(2):
+                reduce_3(l + 1, part)
     store(i).start()
-    reduce_3(0)
+    for part in range(2):
+        reduce_3(0, part)
     for l in reversed(range(depth)):
-        reduce_4(l)
+        for part in range(2):
+            reduce_4(l, part)
 
     for i in range(images):
         store(i).wait()
 
         @pl.when(sends_on)
         def _():
-            message(i).wait_send()
+            for at in range(pieces):
+                message(i, at).wait_send()
 
     for l in range(depth):
-        swap_cores(l).wait_send()
-        swap_cols(l).wait_send()
-        for hop in range(1, depths):
-            swap_rows(l, hop).wait_send()
-
-
-def hand_over(starts, weight_grad, bias_grad, starts_out, weight_out, bias_out, held, in_sem, out_sem):
+        for part in range(2):
+            swap_cores(l, part).wait_send()
+            swap_cols(l, part).wait_send()
+            for hop in range(1, depths):
+                swap_rows(l, part, hop).wait_send()
+
+
+def hand_over(starts, weight_grad, bias_grad, starts_out, weight_out, bias_out, a, b, c, in_sem, out_sem):
     images, pairs = starts.shape[1:3]
     parts = 4 if pairs % 4 == 0 else 1
     some = pairs // parts
-    loads, stores = [], []
+    ways = [(weight_grad, b, weight_out), (bias_grad, c, bias_out)]
     for i in range(images):
         for part in range(parts):
-            at, n = (0, i, pl.ds(part * some, some)), i * parts + part
-            loads.append(pltpu.make_async_copy(starts.at[at], held.at[at], in_sem.at[n]))
-            stores.append(pltpu.make_async_copy(held.at[at], starts_out.at[at], out_sem.at[n]))
+            at = (0, i, pl.ds(part * some, some))
+            ways.append((starts.at[at], a.at[at], starts_out.at[at]))
+    loads = [pltpu.make_async_copy(way[0], way[1], in_sem.at[n]) for n, way in enumerate(ways)]
+    stores = [pltpu.make_async_copy(way[1], way[2], out_sem.at[n]) for n, way in enumerate(ways)]
     for load in loads:
         load.start()
-    weight_out[...] = weight_grad[...]
-    bias_out[...] = bias_grad[...]
     for load, store in zip(loads, stores):
         load.wait()
         store.start()
@@ -448,8 +474,8 @@
             pltpu.VMEM((depth, depths, tall, ch), f32),
             dma((depth,)), dma((depth, images)), dma((images,)), dma((images,)),
             dma((images, 4)), dma((images, 4)),
-            dma((depth,)), dma((depth,)), dma((depth,)), dma((depth,)),
-            dma((depth, depths)), dma((depth, depths)),
+            dma((depth, 2)), dma((depth, 2)), dma((depth, 2)), dma((depth, 2)),
+            dma((depth, 2, depths)), dma((depth, 2, depths)),
         ],
         compiler_params=pltpu.CompilerParams(
             collective_id=0, has_side_effects=True, vmem_limit_bytes=56 * 1024 * 1024
@@ -471,9 +497,15 @@
             jax.ShapeDtypeStruct(weight_grad.shape, f32),
             jax.ShapeDtypeStruct(bias_grad.shape, f32),
         ),
-        in_specs=[anywhere, vmem, vmem],
-        out_specs=(anywhere, vmem, vmem),
-        scratch_shapes=[pltpu.VMEM(starts.shape, f32), dma((images * 4,)), dma((images * 4,))],
+        in_specs=[anywhere] * 3,
+        out_specs=(anywhere,) * 3,
+        scratch_shapes=[
+            pltpu.VMEM(starts.shape, f32),
+            pltpu.VMEM(weight_grad.shape, f32),
+            pltpu.VMEM(bias_grad.shape, f32),
+            dma((images * 4 + 2,)),
+            dma((images * 4 + 2,)),
+        ],
         compiler_params=pltpu.CompilerParams(vmem_limit_bytes=60 * 1024 * 1024),
     )(starts, weight_grad, bias_grad)
     return starts.reshape(guesses.shape), weight_grad, bias_grad

time: 60.9 us -> 56.9 us (0.934)
  Pallas kernels: 60.1 us -> 56.1 us
    pallas_call x1, Pallas kernels: 56.4 us -> 53.9 us  [per_device(): pl.pallas_call(functools.partial(kernel, sections, peers, scale), out_sha...]
    pallas_call x1, Pallas kernels: 3.63 us -> 2.18 us  [per_device(): pl.pallas_call(hand_over, out_shape=(jax.ShapeDtypeStruct(starts.shape, f...]
where the time goes in v3:
time: 56.9 us; the launch traced here: 56.7 us
  Pallas kernels  56.1 us (99%)
  between operations  0.64 us (1%)
    pallas_call x1, Pallas kernels, per_device(): pl.pallas_call(functools.partial(kernel, sections, peers, scale), out_sha...  53.9 us
    pallas_call x1, Pallas kernels, per_device(): pl.pallas_call(hand_over, out_shape=(jax.ShapeDtypeStruct(starts.shape, f...  2.18 us

profile of v3, /device:TPU:0, one launch (start us, length us, event | category | flops | bytes accessed | tf_op | source)
XLA Modules:
  0.0 56.7 jit_solution(889526646213560903)
XLA Ops:
  0.6 53.9 %shard_map.76 = (f32[1,2,16,2,32,128]{5,4,3,2,1,0:T(8,128)}, f32[3,72,128]{2,1,0:T(8,128)}, f32[3,8]{1,0:T(4,128)}) custom-call(bf16[3,2,16,2,32,128]{5,4,3,2,1,0:T(8,128)(2,1)} %bitcast.3, bf16[3,1152,128]{2,1,0:T(8,128)(2,1)} %weights.1, f32[3,128]{1,0:T(4,128)} %bias.1, f32[1,2,16,2,32,128]{5,4,3,2,1,0:T(8,128)} %bitcast.4, f32[2,128]{1,0:T(2,128)} %gain.1), custom_call_target="tpu_custom_call" | custom-call | flops 5435817984 | bytes 6291456 | tf_op jit(solution)/shard_map/pallas_call | solution.py:444
  54.5 2.2 %shard_map.77 = (f32[1,2,16,2,32,128]{5,4,3,2,1,0:T(8,128)}, f32[3,72,128]{2,1,0:T(8,128)}, f32[3,8]{1,0:T(4,128)}) custom-call(f32[1,2,16,2,32,128]{5,4,3,2,1,0:T(8,128)} %get-tuple-element.9.starts, f32[3,72,128]{2,1,0:T(8,128)} %get-tuple-element.10.weight_grad, f32[3,8]{1,0:T(4,128)} %get-tuple-element.11.bias_grad), custom_call_target="tpu_custom_call" | custom-call | tf_op jit(solution)/shard_map/pallas_call | solution.py:493

commit v4 on v3

--- a/solution.py
+++ b/solution.py
@@ -87,9 +87,7 @@
 
     bacc[...] = jnp.zeros_like(bacc)
 
-    @pl.loop(0, depth)
-    def _(t):
-        l = depth - 1 - t
+    def prepare(l):
         load_w(l).wait()
         wf[l, 0 : 9 * ch, 0:ch] = w_in[l]
         wf[l, 9 * ch : 12 * ch, 0:ch] = jnp.zeros((3 * ch, ch), jnp.bfloat16)
@@ -271,25 +269,23 @@
         neighbours = sends_on.astype(jnp.int32) + not_last.astype(jnp.int32)
         pl.semaphore_wait(barrier, len(around) + neighbours)
 
-    half = pairs // 2
-
-    def first_pass(i, band):
-        def part_of(extra):
-            cut = min(half + extra, pairs)
-            return (cut, pairs) if band else (0, cut)
+    def first_pass(i, start, stop, prepares):
+        def span_of(extra):
+            return min(start + extra, pairs) if start else 0, min(stop + extra, pairs)
 
         for l in reversed(range(depth)):
-            if band == 0:
+            if prepares:
+                prepare(l)
+            if start == 0:
                 load_x(l, i).wait()
-            field_step(l, i, *part_of(l + 2))
-            slope_step(l, i, *part_of(l + 1))
-            scale_step(l, i, *part_of(l + 1))
-            adjoint_step(l, i, *part_of(l))
-
-    def send_band(i, band):
+            field_step(l, i, *span_of(l + 2))
+            slope_step(l, i, *span_of(l + 1))
+            scale_step(l, i, *span_of(l + 1))
+            adjoint_step(l, i, *span_of(l))
+
+    def send_band(i, start, stop):
         factor = gain[pl.ds(section - 1, 1), :].reshape(1, 1, 1, ch)
-        count = pieces // 2
-        for at in range(band * count, (band + 1) * count):
+        for at in range(start // piece, stop // piece):
             rows = slice(at * piece, (at + 1) * piece)
 
             @pl.when(not_last)
@@ -302,22 +298,29 @@
 
     @pl.when(sends_on)
     def _():
-        @pl.loop(0, images)
+        load_g(0).wait()
+        adj[0] = g_in[0]
+        bands = [(0, piece), (piece, 2 * piece), (2 * piece, pairs)]
+        for start, stop in bands:
+            first_pass(0, start, stop, start == 0)
+            if start == 0:
+                all_here()
+            send_band(0, start, stop)
+
+        @pl.loop(1, images)
         def _(i):
             load_g(i).wait()
             adj[i] = g_in[i]
-            first_pass(i, 0)
-
-            @pl.when(i == 0)
-            def _():
-                all_here()
-
-            send_band(i, 0)
-            first_pass(i, 1)
-            send_band(i, 1)
+            for start, stop in ((0, 2 * piece), (2 * piece, pairs)):
+                first_pass(i, start, stop, False)
+                send_band(i, start, stop)
 
     @pl.when(jnp.logical_not(sends_on))
     def _():
+        @pl.loop(0, depth)
+        def _(l):
+            prepare(l)
+
         @pl.loop(0, images)
         def _(i):
             load_g(i).wait()
@@ -337,21 +340,21 @@
         def _(l):
             turn_step(l, i)
 
-    def begin(i):
+    def begin(i, start, stop):
         @pl.when(section == 0)
         def _():
-            for at in range(pieces):
+            for at in range(start // piece, stop // piece):
                 message(i, at).wait_recv()
 
         @pl.when(not_last)
         def _():
-            adj[i] = got[i]
+            adj[i, start:stop] = got[i, start:stop]
 
     def store(i):
         return pltpu.make_async_copy(adj.at[i], starts.at[0, i], o_sem.at[i])
 
     for i in range(images - 1):
-        begin(i)
+        begin(i, 0, pairs)
 
         @pl.loop(0, depth)
         def _(t):
@@ -367,11 +370,18 @@
         store(i).start()
 
     i = images - 1
-    begin(i)
-    for l in reversed(range(depth)):
+    for start, stop in ((0, 3 * piece), (3 * piece, pairs)):
+        begin(i, start, stop)
+
         @pl.when(not_last)
         def _():
-            scale_step(l, i, 0, pairs)
+            scale_step(depth - 1, i, start, stop)
+
+    for l in reversed(range(depth)):
+        if l < depth - 1:
+            @pl.when(not_last)
+            def _():
+                scale_step(l, i, 0, pairs)
 
         grad_step(l, i, i == 0)
         reduce_1(l)

time: 56.9 us -> 56.1 us (0.986)
  Pallas kernels: 56.1 us -> 55.1 us
    pallas_call x1, Pallas kernels: 53.9 us -> 52.9 us  [per_device(): pl.pallas_call(functools.partial(kernel, sections, peers, scale), out_sha...]
where the time goes in v4:
time: 56.1 us; the launch traced here: 55.9 us
  Pallas kernels  55.1 us (98%)
  between operations  0.8 us (1%)
    pallas_call x1, Pallas kernels, per_device(): pl.pallas_call(functools.partial(kernel, sections, peers, scale), out_sha...  52.9 us
    pallas_call x1, Pallas kernels, per_device(): pl.pallas_call(hand_over, out_shape=(jax.ShapeDtypeStruct(starts.shape, f...  2.18 us

profile of v4, /device:TPU:0, one launch (start us, length us, event | category | flops | bytes accessed | tf_op | source)
XLA Modules:
  0.0 55.9 jit_solution(7006714726187643258)
XLA Ops:
  0.6 52.9 %shard_map.76 = (f32[1,2,16,2,32,128]{5,4,3,2,1,0:T(8,128)}, f32[3,72,128]{2,1,0:T(8,128)}, f32[3,8]{1,0:T(4,128)}) custom-call(bf16[3,2,16,2,32,128]{5,4,3,2,1,0:T(8,128)(2,1)} %bitcast.3, bf16[3,1152,128]{2,1,0:T(8,128)(2,1)} %weights.1, f32[3,128]{1,0:T(4,128)} %bias.1, f32[1,2,16,2,32,128]{5,4,3,2,1,0:T(8,128)} %bitcast.4, f32[2,128]{1,0:T(2,128)} %gain.1), custom_call_target="tpu_custom_call" | custom-call | flops 5435817984 | bytes 6291456 | tf_op jit(solution)/shard_map/pallas_call | solution.py:454
  53.5 2.2 %shard_map.77 = (f32[1,2,16,2,32,128]{5,4,3,2,1,0:T(8,128)}, f32[3,72,128]{2,1,0:T(8,128)}, f32[3,8]{1,0:T(4,128)}) custom-call(f32[1,2,16,2,32,128]{5,4,3,2,1,0:T(8,128)} %get-tuple-element.9.starts, f32[3,72,128]{2,1,0:T(8,128)} %get-tuple-element.10.weight_grad, f32[3,8]{1,0:T(4,128)} %get-tuple-element.11.bias_grad), custom_call_target="tpu_custom_call" | custom-call | tf_op jit(solution)/shard_map/pallas_call | solution.py:503

commit v5 on v4

--- a/solution.py
+++ b/solution.py
@@ -43,18 +43,6 @@
     around = [peer(row, col, 1 - core), peer(row, 1 - col, core)]
     around += [peer(lax.rem(row + hop, depths), col, core) for hop in range(1, depths)]
 
-    barrier = pltpu.get_barrier_semaphore()
-    for target in around:
-        pl.semaphore_signal(barrier, inc=1, device_id=target, device_id_type=MESH)
-
-    @pl.when(sends_on)
-    def _():
-        pl.semaphore_signal(barrier, inc=1, device_id={"layer": section - 1}, device_id_type=MESH)
-
-    @pl.when(not_last)
-    def _():
-        pl.semaphore_signal(barrier, inc=1, device_id={"layer": section + 1}, device_id_type=MESH)
-
     def load_w(l):
         return pltpu.make_async_copy(weights.at[l], w_in.at[l], w_sem.at[l])
 
@@ -73,6 +61,18 @@
         for l in reversed(range(depth)):
             load_x(l, i).start()
         load_g(i).start()
+
+    barrier = pltpu.get_barrier_semaphore()
+    for target in around:
+        pl.semaphore_signal(barrier, inc=1, device_id=target, device_id_type=MESH)
+
+    @pl.when(sends_on)
+    def _():
+        pl.semaphore_signal(barrier, inc=1, device_id={"layer": section - 1}, device_id_type=MESH)
+
+    @pl.when(not_last)
+    def _():
+        pl.semaphore_signal(barrier, inc=1, device_id={"layer": section + 1}, device_id_type=MESH)
 
     edge = jnp.zeros((width, 3 * ch), jnp.bfloat16)
     for l in range(depth):
@@ -157,17 +157,21 @@
         for j in range(2):
             xt[l, i, :, j * pairs * width : (j + 1) * pairs * width] = flat[j].T
 
-    def grad_step(l, i, first):
-        rows = []
+    def grad_step(l, i, lo, hi, first):
+        rows, left = [], []
         for j in range(2):
             parts = []
             for dy in range(3):
                 r = j + 2 - dy
-                parts.append(s3[l, i, pl.ds(r // 2, pairs), r % 2, :, ch : 2 * ch])
-            rows.append(jnp.concatenate(parts, axis=-1).reshape(pairs * width, 3 * ch))
+                parts.append(s3[l, i, pl.ds(lo + r // 2, hi - lo), r % 2, :, ch : 2 * ch])
+            rows.append(jnp.concatenate(parts, axis=-1).reshape((hi - lo) * width, 3 * ch))
+            left.append(xt[l, i, :, (j * pairs + lo) * width : (j * pairs + hi) * width])
         right = jnp.concatenate(rows, axis=0)
         out = lax.dot_general(
-            xt[l, i], right, (((1,), (0,)), ((), ())), preferred_element_type=jnp.float32
+            jnp.concatenate(left, axis=1),
+            right,
+            (((1,), (0,)), ((), ())),
+            preferred_element_type=jnp.float32,
         )
         total = jnp.sum(right[:, ch : 2 * ch].astype(jnp.float32), axis=0, keepdims=True)
         bacc[pl.ds(l, 1), :] = bacc[pl.ds(l, 1), :] + total
@@ -365,31 +369,40 @@
                 scale_step(l, i, 0, pairs)
                 adjoint_step(l, i, 0, pairs)
 
-            grad_step(l, i, i == 0)
+            grad_step(l, i, 0, pairs, i == 0)
 
         store(i).start()
 
     i = images - 1
-    for start, stop in ((0, 3 * piece), (3 * piece, pairs)):
-        begin(i, start, stop)
+    bands = [(0, 2 * piece), (2 * piece, 3 * piece), (3 * piece, pairs)]
+    middle = 2 * piece
+
+    def second_pass(l, start, stop, step):
+        late = depth - 1 - l + step
+
+        def within(at):
+            return at if at in (0, pairs) else at - late
 
         @pl.when(not_last)
         def _():
-            scale_step(depth - 1, i, start, stop)
-
+            (adjoint_step if step else scale_step)(l, i, within(start), within(stop))
+
+    for start, stop in bands[:-1]:
+        begin(i, start, stop)
+        for l in reversed(range(depth)):
+            second_pass(l, start, stop, 0)
+            if start:
+                grad_step(l, i, 0, middle, i == 0)
+            second_pass(l, start, stop, 1)
+
+    start, stop = bands[-1]
+    begin(i, start, stop)
     for l in reversed(range(depth)):
-        if l < depth - 1:
-            @pl.when(not_last)
-            def _():
-                scale_step(l, i, 0, pairs)
-
-        grad_step(l, i, i == 0)
+        second_pass(l, start, stop, 0)
+        grad_step(l, i, middle, pairs, False)
         reduce_1(l)
 
-        @pl.when(not_last)
-        def _():
-            adjoint_step(l, i, 0, pairs)
-
+        second_pass(l, start, stop, 1)
         for part in range(2):
             reduce_2(l, part)
         if l < depth - 1:

time: 56.1 us -> 55.5 us (0.989)
  Pallas kernels: 55.1 us -> 54.5 us
where the time goes in v5:
time: 55.5 us; the launch traced here: 55.3 us
  Pallas kernels  54.5 us (98%)
  between operations  0.8 us (1%)
    pallas_call x1, Pallas kernels, per_device(): pl.pallas_call(functools.partial(kernel, sections, peers, scale), out_sha...  52.3 us
    pallas_call x1, Pallas kernels, per_device(): pl.pallas_call(hand_over, out_shape=(jax.ShapeDtypeStruct(starts.shape, f...  2.18 us

profile of v5, /device:TPU:0, one launch (start us, length us, event | category | flops | bytes accessed | tf_op | source)
XLA Modules:
  0.0 55.3 jit_solution(8442757159475865141)
XLA Ops:
  0.6 52.3 %shard_map.76 = (f32[1,2,16,2,32,128]{5,4,3,2,1,0:T(8,128)}, f32[3,72,128]{2,1,0:T(8,128)}, f32[3,8]{1,0:T(4,128)}) custom-call(bf16[3,2,16,2,32,128]{5,4,3,2,1,0:T(8,128)(2,1)} %bitcast.3, bf16[3,1152,128]{2,1,0:T(8,128)(2,1)} %weights.1, f32[3,128]{1,0:T(4,128)} %bias.1, f32[1,2,16,2,32,128]{5,4,3,2,1,0:T(8,128)} %bitcast.4, f32[2,128]{1,0:T(2,128)} %gain.1), custom_call_target="tpu_custom_call" | custom-call | flops 5435817984 | bytes 6291456 | tf_op jit(solution)/shard_map/pallas_call | solution.py:467
  53.0 2.2 %shard_map.77 = (f32[1,2,16,2,32,128]{5,4,3,2,1,0:T(8,128)}, f32[3,72,128]{2,1,0:T(8,128)}, f32[3,8]{1,0:T(4,128)}) custom-call(f32[1,2,16,2,32,128]{5,4,3,2,1,0:T(8,128)} %get-tuple-element.9.starts, f32[3,72,128]{2,1,0:T(8,128)} %get-tuple-element.10.weight_grad, f32[3,8]{1,0:T(4,128)} %get-tuple-element.11.bias_grad), custom_call_target="tpu_custom_call" | custom-call | tf_op jit(solution)/shard_map/pallas_call | solution.py:516

commit v6 on v5

--- a/solution.py
+++ b/solution.py
@@ -9,6 +9,7 @@
 
 MESH = pl.DeviceIdType.MESH
 step_size = 0.5
+parts = 3
 
 
 def round_up(value, multiple):
@@ -75,7 +76,11 @@
         pl.semaphore_signal(barrier, inc=1, device_id={"layer": section + 1}, device_id_type=MESH)
 
     edge = jnp.zeros((width, 3 * ch), jnp.bfloat16)
+    blank = jnp.zeros((3 * ch, ch), jnp.bfloat16)
     for l in range(depth):
+        for kernels in (wf, wt):
+            kernels[l, 9 * ch : 12 * ch, 0:ch] = blank
+            kernels[l, 0 : 3 * ch, ch : 2 * ch] = blank
         for i in range(images):
             for field in (x3, s3):
                 field[l, i, 0, 0] = edge
@@ -90,8 +95,6 @@
     def prepare(l):
         load_w(l).wait()
         wf[l, 0 : 9 * ch, 0:ch] = w_in[l]
-        wf[l, 9 * ch : 12 * ch, 0:ch] = jnp.zeros((3 * ch, ch), jnp.bfloat16)
-        wf[l, 0 : 3 * ch, ch : 2 * ch] = jnp.zeros((3 * ch, ch), jnp.bfloat16)
         wf[l, 3 * ch : 12 * ch, ch : 2 * ch] = w_in[l]
         for tap in range(9):
             turned = w_in[l, tap * ch : (tap + 1) * ch, :].T
@@ -99,8 +102,6 @@
             for j in range(2):
                 at = ((dy + j) * 3 + dx) * ch
                 wt[l, at : at + ch, j * ch : (j + 1) * ch] = turned
-        wt[l, 9 * ch : 12 * ch, 0:ch] = jnp.zeros((3 * ch, ch), jnp.bfloat16)
-        wt[l, 0 : 3 * ch, ch : 2 * ch] = jnp.zeros((3 * ch, ch), jnp.bfloat16)
 
     column = lax.broadcasted_iota(jnp.int32, (1, width, ch), 1)
     leftmost, rightmost = column == 0, column == width - 1
@@ -197,8 +198,8 @@
         return padded if l else g.shape[4]
 
     def span(l, part):
-        cut = round_up(padded // 2, 8)
-        return slice(cut, height(l)) if part else slice(0, cut)
+        cut = round_up(-(-padded // parts), 8)
+        return slice(part * cut, (part + 1) * cut if part < parts - 1 else height(l))
 
     def swap_cores(l, part):
         return pltpu.make_async_remote_copy(
@@ -236,7 +237,7 @@
             g[at + (slice(0, block),)] = wacc[l, d * block : (d + 1) * block, :]
             if l == 0:
                 g[at + (slice(padded, None),)] = bacc[...]
-        for part in range(2):
+        for part in range(parts):
             swap_cores(l, part).start()
 
     def reduce_2(l, part):
@@ -261,7 +262,7 @@
             total = total + r3[l, hop - 1, n]
         last = min(n.stop, block)
         weight_grad[l, n.start : last] = scale * total[0 : last - n.start]
-        if l == 0 and part == 1:
+        if l == 0 and part == parts - 1:
             sums = total[padded - n.start : padded - n.start + depth]
             lane = lax.broadcasted_iota(jnp.int32, sums.shape, 1)
             share = bias_grad.shape[1]
@@ -403,16 +404,16 @@
         reduce_1(l)
 
         second_pass(l, start, stop, 1)
-        for part in range(2):
+        for part in range(parts):
             reduce_2(l, part)
         if l < depth - 1:
-            for part in range(2):
+            for part in range(parts):
                 reduce_3(l + 1, part)
     store(i).start()
-    for part in range(2):
+    for part in range(parts):
         reduce_3(0, part)
     for l in reversed(range(depth)):
-        for part in range(2):
+        for part in range(parts):
             reduce_4(l, part)
 
     for i in range(images):
@@ -424,7 +425,7 @@
                 message(i, at).wait_send()
 
     for l in range(depth):
-        for part in range(2):
+        for part in range(parts):
             swap_cores(l, part).wait_send()
             swap_cols(l, part).wait_send()
             for hop in range(1, depths):
@@ -433,12 +434,12 @@
 
 def hand_over(starts, weight_grad, bias_grad, starts_out, weight_out, bias_out, a, b, c, in_sem, out_sem):
     images, pairs = starts.shape[1:3]
-    parts = 4 if pairs % 4 == 0 else 1
-    some = pairs // parts
+    slabs = 4 if pairs % 4 == 0 else 1
+    some = pairs // slabs
     ways = [(weight_grad, b, weight_out), (bias_grad, c, bias_out)]
     for i in range(images):
-        for part in range(parts):
-            at = (0, i, pl.ds(part * some, some))
+        for slab in range(slabs):
+            at = (0, i, pl.ds(slab * some, some))
             ways.append((starts.at[at], a.at[at], starts_out.at[at]))
     loads = [pltpu.make_async_copy(way[0], way[1], in_sem.at[n]) for n, way in enumerate(ways)]
     stores = [pltpu.make_async_copy(way[1], way[2], out_sem.at[n]) for n, way in enumerate(ways)]
@@ -497,8 +498,8 @@
             pltpu.VMEM((depth, depths, tall, ch), f32),
             dma((depth,)), dma((depth, images)), dma((images,)), dma((images,)),
             dma((images, 4)), dma((images, 4)),
-            dma((depth, 2)), dma((depth, 2)), dma((depth, 2)), dma((depth, 2)),
-            dma((depth, 2, depths)), dma((depth, 2, depths)),
+            dma((depth, parts)), dma((depth, parts)), dma((depth, parts)), dma((depth, parts)),
+            dma((depth, parts, depths)), dma((depth, parts, depths)),
         ],
         compiler_params=pltpu.CompilerParams(
             collective_id=0, has_side_effects=True, vmem_limit_bytes=56 * 1024 * 1024

time: 55.5 us -> 55.9 us (level)
  no operation moved by 1% of the time
where the time goes in v6:
time: 55.9 us; the launch traced here: 55.7 us
  Pallas kernels  54.9 us (98%)
  between operations  0.8 us (1%)
    pallas_call x1, Pallas kernels, per_device(): pl.pallas_call(functools.partial(kernel, sections, peers, scale), out_sha...  52.8 us
    pallas_call x1, Pallas kernels, per_device(): pl.pallas_call(hand_over, out_shape=(jax.ShapeDtypeStruct(starts.shape, f...  2.18 us

profile of v6, /device:TPU:0, one launch (start us, length us, event | category | flops | bytes accessed | tf_op | source)
XLA Modules:
  0.0 55.7 jit_solution(14849624776924382793)
XLA Ops:
  0.6 52.8 %shard_map.76 = (f32[1,2,16,2,32,128]{5,4,3,2,1,0:T(8,128)}, f32[3,72,128]{2,1,0:T(8,128)}, f32[3,8]{1,0:T(4,128)}) custom-call(bf16[3,2,16,2,32,128]{5,4,3,2,1,0:T(8,128)(2,1)} %bitcast.3, bf16[3,1152,128]{2,1,0:T(8,128)(2,1)} %weights.1, f32[3,128]{1,0:T(4,128)} %bias.1, f32[1,2,16,2,32,128]{5,4,3,2,1,0:T(8,128)} %bitcast.4, f32[2,128]{1,0:T(2,128)} %gain.1), custom_call_target="tpu_custom_call" | custom-call | flops 5435817984 | bytes 6291456 | tf_op jit(solution)/shard_map/pallas_call | solution.py:468
  53.4 2.2 %shard_map.77 = (f32[1,2,16,2,32,128]{5,4,3,2,1,0:T(8,128)}, f32[3,72,128]{2,1,0:T(8,128)}, f32[3,8]{1,0:T(4,128)}) custom-call(f32[1,2,16,2,32,128]{5,4,3,2,1,0:T(8,128)} %get-tuple-element.9.starts, f32[3,72,128]{2,1,0:T(8,128)} %get-tuple-element.10.weight_grad, f32[3,8]{1,0:T(4,128)} %get-tuple-element.11.bias_grad), custom_call_target="tpu_custom_call" | custom-call | tf_op jit(solution)/shard_map/pallas_call | solution.py:517
